TPU v7x, 256 devices: a whole 4x4x8 slice. The times are simulated.
256 devices in a mesh: row: 32 (over x, y, core), col: 8 (over z).
Axes of the slice: x: 4, y: 4, z: 8, core: 2. Of those that a mesh axis runs over, the one named last changes fastest.
Arguments:
- activations: bfloat16 [512, 16384], P('row', 'col'), may hold values from -6 to 6
- output_gradient: bfloat16 [512, 16384], P('row', 'col'), may hold values from -6 to 6
- frozen_gate_weight: bfloat16 [16384, 26624], P('col', 'row'), may hold values from -0.046875 to 0.046875
- frozen_up_weight: bfloat16 [16384, 26624], P('col', 'row'), may hold values from -0.046875 to 0.046875
- frozen_down_weight: bfloat16 [26624, 16384], P('row', 'col'), may hold values from -0.0390625 to 0.0390625
- gate_adapter_first: bfloat16 [16384, 64], P('col'), may hold values from -0.046875 to 0.046875
- gate_adapter_second: bfloat16 [64, 26624], P(None, 'row'), may hold values from -0.75 to 0.75
- up_adapter_first: bfloat16 [16384, 64], P('col'), may hold values from -0.046875 to 0.046875
- up_adapter_second: bfloat16 [64, 26624], P(None, 'row'), may hold values from -0.75 to 0.75
- down_adapter_first: bfloat16 [26624, 64], P('row'), may hold values from -0.0390625 to 0.0390625
- down_leave: bfloat16 [64, 16384], P(None, 'col'), may hold values from -0.75 to 0.75
Outputs:
- activation_gradient: bfloat16 [512, 16384], P('row', 'col')
- gate_adapter_first_gradient: float32 [16384, 64], P(('col', 'row'))
- gate_adapter_second_gradient: float32 [64, 26624], P(None, 'row')
- up_adapter_first_gradient: float32 [16384, 64], P(('col', 'row'))
- up_adapter_second_gradient: float32 [64, 26624], P(None, 'row')
- down_adapter_first_gradient: float32 [26624, 64], P('row')
- down_adapter_second_gradient: float32 [64, 16384], P(None, ('col', 'row'))
All inputs are finite; a program needn't handle non-finite values.
Results may differ from a plain program's by a relative error of at most 0.028.
Values may be sent and summed in bfloat16 or wider, within the bound.
No kernel may reach another device: no remote copies, remote signals or barrier semaphores. Data moves between devices by JAX's collectives and lax.ppermute only.
A program may use at most 128 MiB of HBM per device.

v0:
```python
import jax
import jax.numpy as jnp
from jax import lax
from jax.sharding import PartitionSpec as P

adapter_scale = 0.5


def matrix_multiply(left, right):
    return jnp.dot(left, right, preferred_element_type=jnp.float32)


def multiply_right_transposed(left, right):
    return lax.dot_general(
        left, right, (((1,), (1,)), ((), ())), preferred_element_type=jnp.float32
    )


def multiply_left_transposed(left, right):
    return lax.dot_general(
        left, right, (((0,), (0,)), ((), ())), preferred_element_type=jnp.float32
    )


def pointwise(gate_activation, up_activation, backward_result):
    sigmoid_gate = jax.nn.sigmoid(gate_activation)
    silu_gate = gate_activation * sigmoid_gate
    hidden_state = (silu_gate * up_activation).astype(jnp.bfloat16)
    up_gradient_term = (backward_result * silu_gate).astype(jnp.bfloat16)
    gate_gradient_term = (
        backward_result
        * up_activation
        * sigmoid_gate
        * (1.0 + gate_activation * (1.0 - sigmoid_gate))
    ).astype(jnp.bfloat16)
    return (hidden_state, gate_gradient_term, up_gradient_term)


def body(
    activations,
    output_gradient,
    frozen_gate_weight,
    frozen_up_weight,
    frozen_down_weight,
    gate_adapter_first,
    gate_adapter_second,
    up_adapter_first,
    up_adapter_second,
    down_adapter_first,
    down_leave,
):
    full_act, full_out = (
        lax.all_gather(activations, "row", axis=0, tiled=True),
        lax.all_gather(output_gradient, "row", axis=0, tiled=True),
    )
    tokens_all = full_act.shape[0]
    width_cols = full_act.shape[1]
    rank = gate_adapter_first.shape[1]
    col_count = lax.axis_size("col")
    row_count = lax.axis_size("row")
    rank_terms = (
        lax.psum(matrix_multiply(full_act, gate_adapter_first).astype(jnp.bfloat16), "col").astype(
            jnp.float32
        ),
        lax.psum(matrix_multiply(full_act, up_adapter_first).astype(jnp.bfloat16), "col").astype(
            jnp.float32
        ),
        lax.psum(
            multiply_right_transposed(full_out, down_leave).astype(jnp.bfloat16), "col"
        ).astype(jnp.float32),
    )
    gate_rank_product = rank_terms[0].astype(jnp.bfloat16)
    up_rank_product = rank_terms[1].astype(jnp.bfloat16)
    down_rank_product = rank_terms[2].astype(jnp.bfloat16)
    share_rows = tokens_all // col_count
    reduced_totals = lax.psum_scatter(
        jnp.stack(
            [
                matrix_multiply(full_act, frozen_gate_weight),
                matrix_multiply(full_act, frozen_up_weight),
                multiply_right_transposed(full_out, frozen_down_weight),
            ],
            axis=1,
        ),
        "col",
        scatter_dimension=0,
        tiled=True,
    )
    first_row = lax.axis_index("col") * share_rows
    gate_row_block = lax.dynamic_slice_in_dim(gate_rank_product, first_row, share_rows, 0)
    up_row_block = lax.dynamic_slice_in_dim(up_rank_product, first_row, share_rows, 0)
    down_row_slice = lax.dynamic_slice_in_dim(down_rank_product, first_row, share_rows, 0)
    gate_activation = reduced_totals[:, 0] + adapter_scale * matrix_multiply(
        gate_row_block, gate_adapter_second
    )
    up_activation = reduced_totals[:, 1] + adapter_scale * matrix_multiply(
        up_row_block, up_adapter_second
    )
    backward_result = reduced_totals[:, 2] + adapter_scale * multiply_right_transposed(
        down_row_slice, down_adapter_first
    )
    hidden_state, gate_gradient_term, up_gradient_term = pointwise(
        gate_activation, up_activation, backward_result
    )
    packed = jnp.stack([hidden_state, gate_gradient_term, up_gradient_term], axis=1)
    piece = lax.all_gather(packed, "col", axis=0, tiled=True)
    piece_hidden = piece[:, 0]
    piece_gate = piece[:, 1]
    piece_up = piece[:, 2]
    rows_input = multiply_right_transposed(
        piece_gate, frozen_gate_weight
    ) + multiply_right_transposed(piece_up, frozen_up_weight)
    rows_factor = jnp.concatenate(
        [
            matrix_multiply(piece_hidden, down_adapter_first),
            multiply_right_transposed(piece_gate, gate_adapter_second),
            multiply_right_transposed(piece_up, up_adapter_second),
        ],
        axis=1,
    )
    input_part = rows_input
    factor_part = rows_factor
    collected_tokens = piece
    input_part, factor_part, collected_tokens = (input_part, factor_part, collected_tokens)
    gate_adapter_second_gradient = adapter_scale * multiply_left_transposed(
        gate_rank_product, collected_tokens[:, 1]
    )
    up_adapter_second_gradient = adapter_scale * multiply_left_transposed(
        up_rank_product, collected_tokens[:, 2]
    )
    down_adapter_first_gradient = adapter_scale * multiply_left_transposed(
        collected_tokens[:, 0], down_rank_product
    )
    factors = lax.psum(factor_part.astype(jnp.bfloat16), "row")
    hidden_rank_product = factors[:, :rank]
    gate_backward = factors[:, rank : 2 * rank]
    up_backward = factors[:, 2 * rank :]
    local_portion = lax.psum_scatter(
        input_part.astype(jnp.bfloat16), "row", scatter_dimension=0, tiled=True
    ).astype(jnp.float32)
    share_tokens = tokens_all // row_count
    first_token = lax.axis_index("row") * share_tokens
    gate_row_slice = lax.dynamic_slice_in_dim(gate_backward, first_token, share_tokens, 0)
    up_row_slice = lax.dynamic_slice_in_dim(up_backward, first_token, share_tokens, 0)
    activation_gradient = (
        local_portion
        + adapter_scale
        * (
            multiply_right_transposed(gate_row_slice, gate_adapter_first)
            + multiply_right_transposed(up_row_slice, up_adapter_first)
        )
    ).astype(jnp.bfloat16)
    piece_width = width_cols // row_count
    first_feature = lax.axis_index("row") * piece_width
    activation_columns = lax.dynamic_slice_in_dim(full_act, first_feature, piece_width, 1)
    output_columns = lax.dynamic_slice_in_dim(full_out, first_feature, piece_width, 1)
    gate_adapter_first_gradient = adapter_scale * multiply_left_transposed(
        activation_columns, gate_backward
    )
    up_adapter_first_gradient = adapter_scale * multiply_left_transposed(
        activation_columns, up_backward
    )
    down_adapter_second_gradient = adapter_scale * multiply_left_transposed(
        hidden_rank_product, output_columns
    )
    return (
        activation_gradient,
        gate_adapter_first_gradient,
        gate_adapter_second_gradient,
        up_adapter_first_gradient,
        up_adapter_second_gradient,
        down_adapter_first_gradient,
        down_adapter_second_gradient,
    )


def solution(mesh):
    return jax.shard_map(
        body,
        mesh=mesh,
        in_specs=(
            P("row", "col"),
            P("row", "col"),
            P("col", "row"),
            P("col", "row"),
            P("row", "col"),
            P("col", None),
            P(None, "row"),
            P("col", None),
            P(None, "row"),
            P("row", None),
            P(None, "col"),
        ),
        out_specs=(
            P("row", "col"),
            P(("col", "row"), None),
            P(None, "row"),
            P(("col", "row"), None),
            P(None, "row"),
            P("row", None),
            P(None, ("col", "row")),
        ),
        check_vma=False,
    )
```

profile of v0, /device:TPU:1, one launch (start us, length us, event | category | flops | bytes accessed | tf_op | source)
XLA Modules:
  0.0 628.4 jit_solution(6578935335400134169)
XLA Ops:
  8.7 55.0 %all-gather.4.cloned.1.call-done = bf16[512,2048]{1,0:T(8,128)(2,1)} async-done(((bf16[16,2048]{1,0:T(8,128)(2,1)}), bf16[512,2048]{1,0:T(8,128)(2,1)}) %all-gather.4.cloned.1.call-update) | async-done | bytes 2097168 | tf_op jit(solution)/shard_map/all_gather | solution.py:53
  63.7 5.9 convolution_bitcast_fusion.1
  69.6 3.2 convolution_bitcast_fusion.2
  72.8 41.6 %all-gather.6.cloned.1.call-done = bf16[512,2048]{1,0:T(8,128)(2,1)} async-done(((bf16[16,2048]{1,0:T(8,128)(2,1)}), bf16[512,2048]{1,0:T(8,128)(2,1)}) %all-gather.6.cloned.1.call-update) | async-done | bytes 2097168 | tf_op jit(solution)/shard_map/all_gather | solution.py:54
  114.4 4.7 convolution_bitcast_fusion
  119.1 2.8 pad_maximum_fusion
  121.9 8.3 %copy.25 = f32[512,3,832]{2,1,0:T(4,128)} copy(f32[512,3,832]{0,2,1:T(8,128)} %pad_maximum_fusion) | data formatting | bytes 10223616 | tf_op jit(solution)/shard_map/stack | solution.py:77
  130.3 3.1 convolution_convert_fusion.3
  133.4 3.0 convolution_convert_fusion.5
  139.2 158.3 %all-reduce.8.cloned.1.call-done = f32[512,3,832]{2,1,0:T(4,128)} async-done(((f32[512,3,832]{2,1,0:T(4,128)}), f32[512,3,832]{2,1,0:T(4,128)}) %all-reduce.8.cloned.1.call-update) | async-done | bytes 5111824
  297.5 3.3 constant_dynamic-slice_fusion
  300.8 65.8 %all-reduce.10.cloned.1.call-done = (bf16[512,64]{0,1:T(8,128)(2,1)}, bf16[512,64]{0,1:T(8,128)(2,1)}, bf16[512,64]{0,1:T(8,128)(2,1)}) async-done(((bf16[512,64]{0,1:T(8,128)(2,1)}, bf16[512,64]{0,1:T(8,128)(2,1)}, bf16[512,64]{0,1:T(8,128)(2,1)}), (bf16[512,64]{0,1:T(8,128)(2,1)}, bf16[512,64]{0,1:T(8,128)(2,1)}, bf16[512,64]{0,1:T(8,128)(2,1)})) %all-reduce.10.cloned.1.call-update) | async-done | bytes 196624 | tf_op jit(solution)/shard_map/psum | solution.py:68
  371.5 43.8 %all-gather.8.cloned.1.call-done = bf16[512,3,832]{2,0,1:T(8,128)(2,1)} async-done(((bf16[64,3,832]{2,0,1:T(8,128)(2,1)}), bf16[512,3,832]{2,0,1:T(8,128)(2,1)}) %all-gather.8.cloned.1.call-update) | async-done | bytes 2555920 | tf_op jit(solution)/shard_map/all_gather | solution.py:106
  421.0 3.7 fusion.6
  424.7 4.9 add_convert_fusion
  429.6 2.2 convolution_multiply_fusion.5
  431.8 2.2 convolution_multiply_fusion.4
  434.0 2.2 convolution_multiply_fusion.3
  436.1 95.4 %all-reduce.6.cloned.1.call-done = bf16[512,192]{0,1:T(8,128)(2,1)} async-done(((bf16[512,192]{0,1:T(8,128)(2,1)}), bf16[512,192]{0,1:T(8,128)(2,1)}) %all-reduce.6.cloned.1.call-update) | async-done | bytes 196624 | tf_op jit(solution)/shard_map/psum | solution.py:134
  531.5 1.8 convolution_multiply_fusion.8
  533.3 1.8 convolution_multiply_fusion.7
  535.1 1.8 convolution_multiply_fusion.6
  539.6 80.0 %reduce-scatter.2.cloned.1.call-done = bf16[16,2048]{1,0:T(8,128)(2,1)} async-done(((bf16[512,2048]{1,0:T(8,128)(2,1)}), bf16[16,2048]{1,0:T(8,128)(2,1)}) %reduce-scatter.2.cloned.1.call-update) | async-done | bytes 65552 | tf_op jit(solution)/shard_map/reduce_scatter | solution.py:138
  619.7 1.9 fusion.2
  (48 shorter events, 16.8 us)
Async XLA Ops:
  7.2 62.4 %copy-start = (bf16[2048,832]{0,1:T(8,128)(2,1)S(1)}, bf16[2048,832]{0,1:T(8,128)(2,1)}, u32[]{:S(2)}) copy-start(bf16[2048,832]{0,1:T(8,128)(2,1)} %param.13) | copy-start | bytes 10223620
  7.2 56.5 %all-gather.4.cloned.1.call-start = ((), (), s32[]{:S(2)}) async-start(), calls=%async_computation.1 | async-start | bytes 2162688 | tf_op jit(solution)/shard_map/all_gather | solution.py:53
  7.9 106.5 %all-gather.6.cloned.1.call-start = ((), (), s32[]{:S(2)}) async-start(), calls=%async_computation.2 | async-start | bytes 2162688 | tf_op jit(solution)/shard_map/all_gather | solution.py:54
  8.7 288.8 %all-reduce.8.cloned.1.call-start = ((), (), s32[]{:S(2)}) async-start(), calls=%async_computation.6 | async-start | bytes 14680064
  63.7 5.9 copy-start.1
  114.4 4.7 copy-start.3
  114.4 4.7 copy-start.4
  130.2 236.4 %all-reduce.10.cloned.1.call-start = ((), (), s32[]{:S(2)}) async-start(), calls=%async_computation.7 | async-start | bytes 393216 | tf_op jit(solution)/shard_map/psum | solution.py:68
  130.3 6.2 copy-start.2
  130.3 6.2 copy-start.5
  133.4 4.5 copy-start.10
  133.4 233.2 %copy-start.6 = (bf16[64,832]{1,0:T(8,128)(2,1)S(1)}, bf16[64,832]{1,0:T(8,128)(2,1)}, u32[]{:S(2)}) copy-start(bf16[64,832]{1,0:T(8,128)(2,1)} %param.19) | copy-start | bytes 319492
  137.9 277.4 %all-gather.8.cloned.1.call-start = ((), (), s32[]{:S(2)}) async-start(), calls=%async_computation.3 | async-start | bytes 3096576 | tf_op jit(solution)/shard_map/all_gather | solution.py:106
  371.4 160.1 %all-reduce.6.cloned.1.call-start = ((), (), s32[]{:S(2)}) async-start(), calls=%async_computation.5 | async-start | bytes 393216 | tf_op jit(solution)/shard_map/psum | solution.py:134
  420.8 198.9 %reduce-scatter.2.cloned.1.call-start = ((), (), s32[]{:S(2)}) async-start(), calls=%async_computation.4 | async-start | bytes 2162688 | tf_op jit(solution)/shard_map/reduce_scatter | solution.py:138
  421.0 3.7 copy-start.9
  429.6 2.3 copy-start.8
  429.6 4.4 copy-start.7
Sparse Core Ops, SparseCore 0:
  10.6 53.0 all-gather.3
  66.2 48.1 all-gather.5
  130.3 167.1 all-reduce.7
  300.5 66.1 all-reduce.9
  371.5 43.6 all-gather.7
  420.9 110.5 all-reduce.5
  535.3 84.2 reduce-scatter.1
where the time goes:
time: 630 us; the launch traced here: 628 us
  waiting for transfers between devices  541 us (86%)
  matrix products  53.6 us (9%)
  between operations  14.9 us (2%)
  local copies, waits for them, and re-layouts  13.7 us (2%)
    unnamed x8, waiting for transfers between devices  160 us
    psum x1, waiting for transfers between devices, body(): factors = lax.psum(factor_part.astype(jnp.bfloat16), 'row')  95.4 us
    reduce_scatter x1, waiting for transfers between devices, body(): lax.psum_scatter(input_part.astype(jnp.bfloat16), 'row', scatter_dimensio...  80 us
    psum x1, waiting for transfers between devices, body(): lax.psum(multiply_right_transposed(full_out, down_leave).astype(jnp.bfloa...  65.8 us
    all_gather x1, waiting for transfers between devices, body(): lax.all_gather(activations, 'row', axis=0, tiled=True)  55 us
    all_gather x1, waiting for transfers between devices, body(): piece = lax.all_gather(packed, 'col', axis=0, tiled=True)  43.8 us
    all_gather x1, waiting for transfers between devices, body(): lax.all_gather(output_gradient, 'row', axis=0, tiled=True)  41.6 us
    dot_general x9, matrix products, multiply_right_transposed(): lax.dot_general(left, right, (((1,), (1,)), ((), ())), preferred_element_...  23.9 us
  transfers between devices with their start and end apart: 7, of which 7 were waited for; matrix products, arithmetic and copies ran while one was open for 7% of the time, Pallas kernels for 0%

commit v1 on v0

v1 whole, which is shorter than its diff:
```python
import jax
import jax.numpy as jnp
from jax import lax
from jax.sharding import PartitionSpec as P

adapter_scale = 0.5


def matrix_multiply(left, right):
    return jnp.dot(left, right, preferred_element_type=jnp.float32)


def multiply_right_transposed(left, right):
    return lax.dot_general(
        left, right, (((1,), (1,)), ((), ())), preferred_element_type=jnp.float32
    )


def multiply_left_transposed(left, right):
    return lax.dot_general(
        left, right, (((0,), (0,)), ((), ())), preferred_element_type=jnp.float32
    )


def pointwise(gate_activation, up_activation, backward_result):
    sigmoid_gate = jax.nn.sigmoid(gate_activation)
    silu_gate = gate_activation * sigmoid_gate
    hidden_state = (silu_gate * up_activation).astype(jnp.bfloat16)
    up_gradient_term = (backward_result * silu_gate).astype(jnp.bfloat16)
    gate_gradient_term = (
        backward_result
        * up_activation
        * sigmoid_gate
        * (1.0 + gate_activation * (1.0 - sigmoid_gate))
    ).astype(jnp.bfloat16)
    return (hidden_state, gate_gradient_term, up_gradient_term)


def body(
    activations,
    output_gradient,
    frozen_gate_weight,
    frozen_up_weight,
    frozen_down_weight,
    gate_adapter_first,
    gate_adapter_second,
    up_adapter_first,
    up_adapter_second,
    down_adapter_first,
    down_leave,
):
    share_tokens, width = activations.shape
    rank, hidden_units = gate_adapter_second.shape
    row_count = lax.axis_size("row")
    tokens_all = share_tokens * row_count
    packed_width = hidden_units + rank

    both = lax.all_gather(
        jnp.concatenate([activations, output_gradient], axis=1), "row", axis=0, tiled=True
    )
    full_act = both[:, :width]
    full_out = both[:, width:]

    partial = jnp.concatenate(
        [
            matrix_multiply(full_act, frozen_gate_weight).astype(jnp.bfloat16),
            matrix_multiply(full_act, gate_adapter_first).astype(jnp.bfloat16),
            matrix_multiply(full_act, frozen_up_weight).astype(jnp.bfloat16),
            matrix_multiply(full_act, up_adapter_first).astype(jnp.bfloat16),
            multiply_right_transposed(full_out, frozen_down_weight).astype(jnp.bfloat16),
            multiply_right_transposed(full_out, down_leave).astype(jnp.bfloat16),
        ],
        axis=1,
    )
    totals = lax.psum_scatter(partial, "col", scatter_dimension=0, tiled=True)
    wide = [
        totals[:, i * packed_width : i * packed_width + hidden_units].astype(jnp.float32)
        for i in range(3)
    ]
    low = [totals[:, i * packed_width + hidden_units : (i + 1) * packed_width] for i in range(3)]
    gate_activation = wide[0] + adapter_scale * matrix_multiply(low[0], gate_adapter_second)
    up_activation = wide[1] + adapter_scale * matrix_multiply(low[1], up_adapter_second)
    backward_result = wide[2] + adapter_scale * multiply_right_transposed(
        low[2], down_adapter_first
    )
    hidden_state, gate_gradient_term, up_gradient_term = pointwise(
        gate_activation, up_activation, backward_result
    )
    packed = jnp.concatenate(
        [hidden_state, low[2], gate_gradient_term, low[0], up_gradient_term, low[1]], axis=1
    )
    piece = lax.all_gather(packed, "col", axis=0, tiled=True)
    piece_hidden, down_low, piece_gate, gate_low, piece_up, up_low = [
        piece[:, start : start + size]
        for i in range(3)
        for start, size in (
            (i * packed_width, hidden_units),
            (i * packed_width + hidden_units, rank),
        )
    ]

    share = jnp.concatenate(
        [
            (
                multiply_right_transposed(piece_gate, frozen_gate_weight)
                + multiply_right_transposed(piece_up, frozen_up_weight)
            ).astype(jnp.bfloat16),
            matrix_multiply(piece_hidden, down_adapter_first).astype(jnp.bfloat16),
            multiply_right_transposed(piece_gate, gate_adapter_second).astype(jnp.bfloat16),
            multiply_right_transposed(piece_up, up_adapter_second).astype(jnp.bfloat16),
        ],
        axis=1,
    )
    shares = lax.all_to_all(share, "row", 0, 0, tiled=True)
    summed = jnp.sum(
        shares.reshape(row_count, share_tokens, width + 3 * rank).astype(jnp.float32), axis=0
    )
    own_factors = summed[:, width:].astype(jnp.bfloat16)
    factors = lax.all_gather(own_factors, "row", axis=0, tiled=True)
    activation_gradient = (
        summed[:, :width]
        + adapter_scale
        * (
            multiply_right_transposed(own_factors[:, rank : 2 * rank], gate_adapter_first)
            + multiply_right_transposed(own_factors[:, 2 * rank :], up_adapter_first)
        )
    ).astype(jnp.bfloat16)

    gate_adapter_second_gradient = adapter_scale * multiply_left_transposed(gate_low, piece_gate)
    up_adapter_second_gradient = adapter_scale * multiply_left_transposed(up_low, piece_up)
    down_adapter_first_gradient = adapter_scale * multiply_left_transposed(piece_hidden, down_low)

    piece_width = width // row_count
    first_feature = lax.axis_index("row") * piece_width
    activation_columns = lax.dynamic_slice_in_dim(full_act, first_feature, piece_width, 1)
    output_columns = lax.dynamic_slice_in_dim(full_out, first_feature, piece_width, 1)
    gate_adapter_first_gradient = adapter_scale * multiply_left_transposed(
        activation_columns, factors[:, rank : 2 * rank]
    )
    up_adapter_first_gradient = adapter_scale * multiply_left_transposed(
        activation_columns, factors[:, 2 * rank :]
    )
    down_adapter_second_gradient = adapter_scale * multiply_left_transposed(
        factors[:, :rank], output_columns
    )
    return (
        activation_gradient,
        gate_adapter_first_gradient,
        gate_adapter_second_gradient,
        up_adapter_first_gradient,
        up_adapter_second_gradient,
        down_adapter_first_gradient,
        down_adapter_second_gradient,
    )


def solution(mesh):
    return jax.shard_map(
        body,
        mesh=mesh,
        in_specs=(
            P("row", "col"),
            P("row", "col"),
            P("col", "row"),
            P("col", "row"),
            P("row", "col"),
            P("col", None),
            P(None, "row"),
            P("col", None),
            P(None, "row"),
            P("row", None),
            P(None, "col"),
        ),
        out_specs=(
            P("row", "col"),
            P(("col", "row"), None),
            P(None, "row"),
            P(("col", "row"), None),
            P(None, "row"),
            P("row", None),
            P(None, ("col", "row")),
        ),
        check_vma=False,
    )
```

time: 630 us -> 282 us (0.45)
  waiting for transfers between devices: 541 us -> 164 us
  blocking collectives: 0 us -> 23.2 us
  starting transfers between devices: 0.46 us -> 10.3 us
  matrix products: 53.6 us -> 43.8 us
  local copies, waits for them, and re-layouts: 13.7 us -> 21.5 us
    psum x2 -> x0, waiting for transfers between devices: 161 us -> none  [the longest x1 95.4 us: body(): factors = lax.psum(factor_part.astype(jnp.bfloat16), 'row')]
    unnamed x8 -> x3, waiting for transfers between devices: 160 us -> 0.05 us
    reduce_scatter x1, waiting for transfers between devices: 80 us -> 39.9 us  [body(): totals = lax.psum_scatter(partial, 'col', scatter_dimension=0, tiled=True)]
    all_gather x2 -> x1, waiting for transfers between devices: 96.5 us -> 57.5 us  [body(): lax.all_gather(jnp.concatenate([activations, output_gradient], axis=1), '...]
    all_gather x0 -> x1, blocking collectives: none -> 23.2 us  [body(): factors = lax.all_gather(own_factors, 'row', axis=0, tiled=True)]
    all_to_all x0 -> x1, waiting for transfers between devices: none -> 23 us  [body(): shares = lax.all_to_all(share, 'row', 0, 0, tiled=True)]
    all_to_all x0 -> x1, starting transfers between devices: none -> 10 us  [body(): shares = lax.all_to_all(share, 'row', 0, 0, tiled=True)]
    another operation x1 -> x0, local copies, waits for them, and re-layouts: 8.27 us -> none  [body(): jnp.stack([matrix_multiply(full_act, frozen_gate_weight), matrix_multiply...]
  transfers between devices with their start and end apart: 7 -> 4, of which waited for: 7 -> 4; matrix products, arithmetic and copies ran while one was open for 7% -> 3% of each run, Pallas kernels for 0% -> 0%
where the time goes in v1:
time: 282 us; the launch traced here: 281 us
  waiting for transfers between devices  164 us (58%)
  matrix products  43.8 us (16%)
  blocking collectives  23.2 us (8%)
  local copies, waits for them, and re-layouts  21.5 us (8%)
  between operations  13.9 us (5%)
  starting transfers between devices  10.3 us (4%)
  other arithmetic  3.76 us (1%)
    all_gather x1, waiting for transfers between devices, body(): lax.all_gather(jnp.concatenate([activations, output_gradient], axis=1), '...  57.5 us
    all_gather x1, waiting for transfers between devices, body(): piece = lax.all_gather(packed, 'col', axis=0, tiled=True)  44 us
    reduce_scatter x1, waiting for transfers between devices, body(): totals = lax.psum_scatter(partial, 'col', scatter_dimension=0, tiled=True)  39.9 us
    all_gather x1, blocking collectives, body(): factors = lax.all_gather(own_factors, 'row', axis=0, tiled=True)  23.2 us
    all_to_all x1, waiting for transfers between devices, body(): shares = lax.all_to_all(share, 'row', 0, 0, tiled=True)  23 us
    dot_general x9, matrix products, multiply_right_transposed(): lax.dot_general(left, right, (((1,), (1,)), ((), ())), preferred_element_...  20.2 us
    dot_general x7, matrix products, matrix_multiply(): return jnp.dot(left, right, preferred_element_type=jnp.float32)  14.9 us
    all_to_all x1, starting transfers between devices, body(): shares = lax.all_to_all(share, 'row', 0, 0, tiled=True)  10 us
  transfers between devices with their start and end apart: 4, of which 4 were waited for; matrix products, arithmetic and copies ran while one was open for 3% of the time, Pallas kernels for 0%

profile of v1, /device:TPU:1, one launch (start us, length us, event | category | flops | bytes accessed | tf_op | source)
XLA Modules:
  0.0 280.8 jit_solution(5499502897744341676)
XLA Ops:
  7.2 1.7 pad_maximum_fusion
  9.0 57.5 %all-gather.3.cloned.1.call-done = bf16[512,4096]{1,0:T(8,128)(2,1)} async-done(((bf16[16,4096]{1,0:T(8,128)(2,1)}), bf16[512,4096]{1,0:T(8,128)(2,1)}) %all-gather.3.cloned.1.call-update) | async-done | bytes 4194320 | tf_op jit(solution)/shard_map/all_gather | solution.py:58
  66.5 4.6 %fusion.5 = bf16[512,2688]{0,1:T(8,128)(2,1)} fusion(bf16[2048,832]{0,1:T(8,128)(2,1)S(1)} %copy-done, bf16[512,4096]{1,0:T(8,128)(2,1)} %all-gather.3.cloned.1.call-done), kind=kOutput, calls=%fused_computation.11 | convolution fusion | flops 1745256448 | bytes 6356992 | tf_op jit(solution)/shard_map/dot_general | solution.py:10
  72.5 2.9 %fusion.4 = bf16[512,2688]{0,1:T(8,128)(2,1)} fusion(bf16[512,2688]{0,1:T(8,128)(2,1)} %fusion.9, bf16[2048,832]{0,1:T(8,128)(2,1)S(1)} %copy-done.9, bf16[512,4096]{1,0:T(8,128)(2,1)S(1)} %copy-done.1), kind=kOutput, calls=%fused_computation.9 | convolution fusion | flops 1745256448 | bytes 6356992 | tf_op jit(solution)/shard_map/dot_general | solution.py:10
  76.8 2.9 %fusion.3 = bf16[512,2688]{0,1:T(8,128)(2,1)} fusion(bf16[512,2688]{0,1:T(8,128)(2,1)} %fusion.10, bf16[832,2048]{1,0:T(8,128)(2,1)S(1)} %copy-done.8, bf16[512,4096]{1,0:T(8,128)(2,1)S(1)} %copy-done.1), kind=kOutput, calls=%fused_computation.7 | convolution fusion | flops 1745256448 | bytes 6356992 | tf_op jit(solution)/shard_map/dot_general | solution.py:14
  81.1 4.5 %copy.46 = bf16[512,2688]{1,0:T(8,128)(2,1)} copy(bf16[512,2688]{0,1:T(8,128)(2,1)} %fusion.11) | data formatting | bytes 5505024
  85.9 39.9 %reduce-scatter.4.cloned.1.call-done = bf16[64,2688]{1,0:T(8,128)(2,1)} async-done(((bf16[512,2688]{1,0:T(8,128)(2,1)}), bf16[64,2688]{1,0:T(8,128)(2,1)}) %reduce-scatter.4.cloned.1.call-update) | async-done | bytes 344080 | tf_op jit(solution)/shard_map/reduce_scatter | solution.py:75
  129.6 1.9 multiply_convert_fusion
  131.6 1.8 concatenate.14
  133.4 44.0 %all-gather.5.cloned.1.call-done = bf16[512,2688]{1,0:T(8,128)(2,1)} async-done(((bf16[64,2688]{1,0:T(8,128)(2,1)}), bf16[512,2688]{1,0:T(8,128)(2,1)}) %all-gather.5.cloned.1.call-update) | async-done | bytes 2752528 | tf_op jit(solution)/shard_map/all_gather | solution.py:92
  177.4 2.2 convolution_convert_fusion.5
  180.6 2.2 convolution_convert_fusion.4
  184.4 2.2 convolution_convert_fusion.3
  188.2 3.7 %fusion.19 = f32[512,2048]{1,0:T(8,128)S(1)} fusion(bf16[2048,832]{0,1:T(8,128)(2,1)S(1)} %copy-done, bf16[512,2688]{1,0:T(8,128)(2,1)} %all-gather.5.cloned.1.call-done), kind=kOutput, calls=%fused_computation.40 | convolution fusion | flops 1744830464 | bytes 8519680 | tf_op jit(solution)/shard_map/dot_general | solution.py:14
  191.9 4.8 %add_convert_fusion = bf16[512,2048]{1,0:T(8,128)(2,1)} fusion(f32[512,2048]{1,0:T(8,128)S(1)} %fusion.19, bf16[2048,832]{0,1:T(8,128)(2,1)S(1)} %copy-done.10, bf16[512,2688]{1,0:T(8,128)(2,1)} %all-gather.5.cloned.1.call-done), kind=kOutput, calls=%fused_computation.1 | convolution fusion | flops 1746927616 | bytes 10616832 | tf_op jit(solution)/shard_map/dot_general | solution.py:14
  196.7 4.6 %concatenate.15 = bf16[512,2240]{1,0:T(8,128)(2,1)} concatenate(bf16[512,2048]{1,0:T(8,128)(2,1)} %add_convert_fusion, bf16[512,64]{1,0:T(8,128)(2,1)S(1)} %copy.43, bf16[512,64]{1,0:T(8,128)(2,1)} %copy.44, bf16[512,64]{1,0:T(8,128)(2,1)} %copy.45), dimensions={1} | concatenate | bytes 4587520 | tf_op jit(solution)/shard_map/concatenate | solution.py:102
  201.3 10.0 %all-to-all-start = ((bf16[32,16,2240]{2,1,0:T(8,128)(2,1)}), bf16[32,16,2240]{2,1,0:T(8,128)(2,1)}, u32[]{:S(2)}, u32[]{:S(2)}) async-start(bf16[32,16,2240]{2,1,0:T(8,128)(2,1)} %bitcast.18), calls=%async_computation | async-start | bytes 4718592 | tf_op jit(solution)/shard_map/all_to_all | solution.py:114
  211.4 4.9 %fusion.46 = (bf16[512,2048]{1,0:T(8,128)(2,1)}, bf16[512,2048]{1,0:T(8,128)(2,1)}) fusion(bf16[512,4096]{1,0:T(8,128)(2,1)} %all-gather.3.cloned.1.call-done), kind=kLoop, calls=%fused_computation.72 | loop fusion | bytes 8388608 | tf_op jit(solution)/shard_map/slice | solution.py:62
  219.6 23.0 %all-to-all-done = bf16[32,16,2240]{2,1,0:T(8,128)(2,1)} async-done(((bf16[32,16,2240]{2,1,0:T(8,128)(2,1)}), bf16[32,16,2240]{2,1,0:T(8,128)(2,1)}, u32[]{:S(2)}, u32[]{:S(2)}) %all-to-all-start) | async-done | bytes 2293792 | tf_op jit(solution)/shard_map/all_to_all | solution.py:114
  242.6 2.1 convert_reduce_fusion
  244.7 23.2 %all_gather.11 = bf16[512,192]{1,0:T(8,128)(2,1)S(1)} all-gather(bf16[16,192]{1,0:T(8,128)(2,1)S(1)} %slice.101), channel_id=1, replica_groups=mesh['row'=32,'col'=8] {'row'}, dimensions={0}, use_global_device_ids=true | all-gather | bytes 202752 | tf_op jit(solution)/shard_map/all_gather | solution.py:119
  267.8 1.8 convolution_multiply_fusion.7
  269.6 1.8 convolution_multiply_fusion.8
  271.6 1.8 convolution_multiply_fusion.6
  (46 shorter events, 16.8 us)
Async XLA Ops:
  7.2 59.3 %copy-start = (bf16[2048,832]{0,1:T(8,128)(2,1)S(1)}, bf16[2048,832]{0,1:T(8,128)(2,1)}, u32[]{:S(2)}) copy-start(bf16[2048,832]{0,1:T(8,128)(2,1)} %param.13) | copy-start | bytes 10223620
  7.2 59.3 %all-gather.3.cloned.1.call-start = ((), (), s32[]{:S(2)}) async-start(), calls=%async_computation.2 | async-start | bytes 4325376 | tf_op jit(solution)/shard_map/all_gather | solution.py:58
  8.9 116.8 %reduce-scatter.4.cloned.1.call-start = ((), (), s32[]{:S(2)}) async-start(), calls=%async_computation.4 | async-start | bytes 3096576 | tf_op jit(solution)/shard_map/reduce_scatter | solution.py:75
  66.5 4.6 %copy-start.1 = (bf16[512,4096]{1,0:T(8,128)(2,1)S(1)}, bf16[512,4096]{1,0:T(8,128)(2,1)}, u32[]{:S(2)}) copy-start(bf16[512,4096]{1,0:T(8,128)(2,1)} %all-gather.3.cloned.1.call-done) | copy-start | bytes 12582916
  66.5 4.6 %copy-start.5 = (bf16[2048,64]{0,1:T(8,128)(2,1)S(1)}, bf16[2048,64]{0,1:T(8,128)(2,1)}, u32[]{:S(2)}) copy-start(bf16[2048,64]{0,1:T(8,128)(2,1)} %param.16) | copy-start | bytes 786436
  66.5 6.0 %copy-start.9 = (bf16[2048,832]{0,1:T(8,128)(2,1)S(1)}, bf16[2048,832]{0,1:T(8,128)(2,1)}, u32[]{:S(2)}) copy-start(bf16[2048,832]{0,1:T(8,128)(2,1)} %param.14) | copy-start | bytes 10223620
  72.5 2.9 %copy-start.3 = (bf16[2048,64]{0,1:T(8,128)(2,1)S(1)}, bf16[2048,64]{0,1:T(8,128)(2,1)}, u32[]{:S(2)}) copy-start(bf16[2048,64]{0,1:T(8,128)(2,1)} %param.18) | copy-start | bytes 786436
  72.5 4.3 %copy-start.8 = (bf16[832,2048]{1,0:T(8,128)(2,1)S(1)}, bf16[832,2048]{1,0:T(8,128)(2,1)}, u32[]{:S(2)}) copy-start(bf16[832,2048]{1,0:T(8,128)(2,1)} %param.15) | copy-start | bytes 10223620
  76.8 2.9 %copy-start.11 = (bf16[64,2048]{1,0:T(8,128)(2,1)S(1)}, bf16[64,2048]{1,0:T(8,128)(2,1)}, u32[]{:S(2)}) copy-start(bf16[64,2048]{1,0:T(8,128)(2,1)} %param.21) | copy-start | bytes 786436
  85.7 42.8 %copy-start.7 = (bf16[64,832]{1,0:T(8,128)(2,1)S(1)}, bf16[64,832]{1,0:T(8,128)(2,1)}, u32[]{:S(2)}) copy-start(bf16[64,832]{1,0:T(8,128)(2,1)} %param.17) | copy-start | bytes 319492
  85.7 91.7 %all-gather.5.cloned.1.call-start = ((), (), s32[]{:S(2)}) async-start(), calls=%async_computation.3 | async-start | bytes 3096576 | tf_op jit(solution)/shard_map/all_gather | solution.py:92
  188.2 3.7 %copy-start.10 = (bf16[2048,832]{0,1:T(8,128)(2,1)S(1)}, bf16[2048,832]{0,1:T(8,128)(2,1)}, u32[]{:S(2)}) copy-start(bf16[2048,832]{0,1:T(8,128)(2,1)} %param.14) | copy-start | bytes 10223620
  201.3 41.2 %all-to-all-start = ((bf16[32,16,2240]{2,1,0:T(8,128)(2,1)}), bf16[32,16,2240]{2,1,0:T(8,128)(2,1)}, u32[]{:S(2)}, u32[]{:S(2)}) async-start(bf16[32,16,2240]{2,1,0:T(8,128)(2,1)} %bitcast.18), calls=%async_computation | async-start | bytes 4718592 | tf_op jit(solution)/shard_map/all_to_all | solution.py:114
  211.4 5.0 %copy-start.2 = (bf16[512,2688]{1,0:T(8,128)(2,1)S(1)}, bf16[512,2688]{1,0:T(8,128)(2,1)}, u32[]{:S(2)}) copy-start(bf16[512,2688]{1,0:T(8,128)(2,1)} %all-gather.5.cloned.1.call-done) | copy-start | bytes 8257540
  242.6 28.9 %copy-start.6 = (bf16[2048,64]{0,1:T(8,128)(2,1)S(1)}, bf16[2048,64]{0,1:T(8,128)(2,1)}, u32[]{:S(2)}) copy-start(bf16[2048,64]{0,1:T(8,128)(2,1)} %param.16) | copy-start | bytes 786436
  242.6 30.9 %copy-start.4 = (bf16[2048,64]{0,1:T(8,128)(2,1)S(1)}, bf16[2048,64]{0,1:T(8,128)(2,1)}, u32[]{:S(2)}) copy-start(bf16[2048,64]{0,1:T(8,128)(2,1)} %param.18) | copy-start | bytes 786436
Sparse Core Ops, SparseCore 0:
  11.1 55.2 all-gather.2
  85.8 39.9 reduce-scatter.3
  133.5 43.8 all-gather.4

commit v2 on v1

--- a/solution.py
+++ b/solution.py
@@ -34,6 +34,33 @@
         * (1.0 + gate_activation * (1.0 - sigmoid_gate))
     ).astype(jnp.bfloat16)
     return (hidden_state, gate_gradient_term, up_gradient_term)
+
+
+def shifted(size, step):
+    return [(i, (i + step) % size) for i in range(size)]
+
+
+def ring_sum(partial, axis, share):
+    size = lax.axis_size(axis)
+    here = lax.axis_index(axis)
+
+    def block(offset):
+        start = lax.rem(here + offset + size, size) * share
+        return lax.dynamic_slice_in_dim(partial, start, share, 0)
+
+    up_steps = size // 2
+    down_steps = size - 1 - up_steps
+    up = block(up_steps).astype(jnp.bfloat16)
+    down = block(-down_steps).astype(jnp.bfloat16)
+    for step in range(1, up_steps + 1):
+        up = lax.ppermute(up, axis, shifted(size, 1))
+        if step <= down_steps:
+            down = lax.ppermute(down, axis, shifted(size, -1))
+        if step < up_steps:
+            up = (up.astype(jnp.float32) + block(up_steps - step)).astype(jnp.bfloat16)
+        if step < down_steps:
+            down = (down.astype(jnp.float32) + block(step - down_steps)).astype(jnp.bfloat16)
+    return up.astype(jnp.float32) + down.astype(jnp.float32) + block(0)
 
 
 def body(
@@ -52,8 +79,11 @@
     share_tokens, width = activations.shape
     rank, hidden_units = gate_adapter_second.shape
     row_count = lax.axis_size("row")
+    col_count = lax.axis_size("col")
     tokens_all = share_tokens * row_count
-    packed_width = hidden_units + rank
+    col_tokens = tokens_all // col_count
+    chips = row_count // 2
+    core = lax.rem(lax.axis_index("row"), 2)
 
     both = lax.all_gather(
         jnp.concatenate([activations, output_gradient], axis=1), "row", axis=0, tiled=True
@@ -61,23 +91,16 @@
     full_act = both[:, :width]
     full_out = both[:, width:]
 
-    partial = jnp.concatenate(
-        [
-            matrix_multiply(full_act, frozen_gate_weight).astype(jnp.bfloat16),
-            matrix_multiply(full_act, gate_adapter_first).astype(jnp.bfloat16),
-            matrix_multiply(full_act, frozen_up_weight).astype(jnp.bfloat16),
-            matrix_multiply(full_act, up_adapter_first).astype(jnp.bfloat16),
-            multiply_right_transposed(full_out, frozen_down_weight).astype(jnp.bfloat16),
-            multiply_right_transposed(full_out, down_leave).astype(jnp.bfloat16),
-        ],
-        axis=1,
-    )
-    totals = lax.psum_scatter(partial, "col", scatter_dimension=0, tiled=True)
-    wide = [
-        totals[:, i * packed_width : i * packed_width + hidden_units].astype(jnp.float32)
-        for i in range(3)
-    ]
-    low = [totals[:, i * packed_width + hidden_units : (i + 1) * packed_width] for i in range(3)]
+    wide = []
+    low = []
+    for left, right in (
+        (full_act, jnp.concatenate([frozen_gate_weight, gate_adapter_first], axis=1).T),
+        (full_act, jnp.concatenate([frozen_up_weight, up_adapter_first], axis=1).T),
+        (full_out, jnp.concatenate([frozen_down_weight, down_leave], axis=0)),
+    ):
+        total = ring_sum(multiply_right_transposed(left, right), "col", col_tokens)
+        wide.append(total[:, :hidden_units])
+        low.append(total[:, hidden_units:].astype(jnp.bfloat16))
     gate_activation = wide[0] + adapter_scale * matrix_multiply(low[0], gate_adapter_second)
     up_activation = wide[1] + adapter_scale * matrix_multiply(low[1], up_adapter_second)
     backward_result = wide[2] + adapter_scale * multiply_right_transposed(
@@ -87,45 +110,73 @@
         gate_activation, up_activation, backward_result
     )
     packed = jnp.concatenate(
-        [hidden_state, low[2], gate_gradient_term, low[0], up_gradient_term, low[1]], axis=1
+        [gate_gradient_term, up_gradient_term, hidden_state, low[0], low[1], low[2]], axis=1
     )
     piece = lax.all_gather(packed, "col", axis=0, tiled=True)
-    piece_hidden, down_low, piece_gate, gate_low, piece_up, up_low = [
-        piece[:, start : start + size]
-        for i in range(3)
-        for start, size in (
-            (i * packed_width, hidden_units),
-            (i * packed_width + hidden_units, rank),
-        )
-    ]
-
-    share = jnp.concatenate(
+
+    own_factors = jnp.concatenate(
         [
-            (
-                multiply_right_transposed(piece_gate, frozen_gate_weight)
-                + multiply_right_transposed(piece_up, frozen_up_weight)
-            ).astype(jnp.bfloat16),
-            matrix_multiply(piece_hidden, down_adapter_first).astype(jnp.bfloat16),
-            multiply_right_transposed(piece_gate, gate_adapter_second).astype(jnp.bfloat16),
-            multiply_right_transposed(piece_up, up_adapter_second).astype(jnp.bfloat16),
+            matrix_multiply(hidden_state, down_adapter_first).astype(jnp.bfloat16),
+            multiply_right_transposed(gate_gradient_term, gate_adapter_second).astype(jnp.bfloat16),
+            multiply_right_transposed(up_gradient_term, up_adapter_second).astype(jnp.bfloat16),
         ],
         axis=1,
     )
-    shares = lax.all_to_all(share, "row", 0, 0, tiled=True)
+    factor_parts = lax.all_to_all(
+        jnp.broadcast_to(own_factors[None], (row_count,) + own_factors.shape),
+        "row",
+        0,
+        0,
+        tiled=True,
+    )
+    summed_factors = jnp.sum(factor_parts.astype(jnp.float32), axis=0).astype(jnp.bfloat16)
+    factors = lax.all_to_all(
+        jnp.broadcast_to(summed_factors[None], (col_count,) + summed_factors.shape),
+        "col",
+        0,
+        0,
+        tiled=True,
+    ).reshape(tokens_all, 3 * rank)
+
+    input_weight = jnp.concatenate([frozen_gate_weight, frozen_up_weight], axis=1)
+    deltas = piece[:, : 2 * hidden_units].reshape(chips, 2, share_tokens, 2 * hidden_units)
+
+    def tokens_of(which):
+        chosen = lax.dynamic_slice_in_dim(deltas, which, 1, 1)
+        return chosen.reshape(chips * share_tokens, 2 * hidden_units)
+
+    other = multiply_right_transposed(tokens_of(1 - core), input_weight).astype(jnp.bfloat16)
+    other = lax.ppermute(other, "row", [(i, i ^ 1) for i in range(row_count)])
+    own = multiply_right_transposed(tokens_of(core), input_weight)
+    share = (own + other.astype(jnp.float32)).astype(jnp.bfloat16)
+    shares = lax.all_to_all(
+        share,
+        "row",
+        0,
+        0,
+        axis_index_groups=[[2 * chip + c for chip in range(chips)] for c in range(2)],
+        tiled=True,
+    )
     summed = jnp.sum(
-        shares.reshape(row_count, share_tokens, width + 3 * rank).astype(jnp.float32), axis=0
-    )
-    own_factors = summed[:, width:].astype(jnp.bfloat16)
-    factors = lax.all_gather(own_factors, "row", axis=0, tiled=True)
+        shares.reshape(chips, share_tokens, width).astype(jnp.float32), axis=0
+    )
+    first_token = lax.axis_index("row") * share_tokens
+    row_factors = lax.dynamic_slice_in_dim(factors, first_token, share_tokens, 0)
     activation_gradient = (
-        summed[:, :width]
+        summed
         + adapter_scale
         * (
-            multiply_right_transposed(own_factors[:, rank : 2 * rank], gate_adapter_first)
-            + multiply_right_transposed(own_factors[:, 2 * rank :], up_adapter_first)
+            multiply_right_transposed(row_factors[:, rank : 2 * rank], gate_adapter_first)
+            + multiply_right_transposed(row_factors[:, 2 * rank :], up_adapter_first)
         )
     ).astype(jnp.bfloat16)
 
+    piece_gate = piece[:, :hidden_units]
+    piece_up = piece[:, hidden_units : 2 * hidden_units]
+    piece_hidden = piece[:, 2 * hidden_units : 3 * hidden_units]
+    gate_low = piece[:, 3 * hidden_units : 3 * hidden_units + rank]
+    up_low = piece[:, 3 * hidden_units + rank : 3 * hidden_units + 2 * rank]
+    down_low = piece[:, 3 * hidden_units + 2 * rank :]
     gate_adapter_second_gradient = adapter_scale * multiply_left_transposed(gate_low, piece_gate)
     up_adapter_second_gradient = adapter_scale * multiply_left_transposed(up_low, piece_up)
     down_adapter_first_gradient = adapter_scale * multiply_left_transposed(piece_hidden, down_low)

time: 282 us -> 220 us (0.78)
  waiting for transfers between devices: 164 us -> 103 us
  starting transfers between devices: 10.3 us -> 52.2 us
  blocking collectives: 23.2 us -> 0 us
  matrix products: 43.8 us -> 31.9 us
  local copies, waits for them, and re-layouts: 21.5 us -> 13.8 us
    reduce_scatter x1 -> x0, waiting for transfers between devices: 39.9 us -> none  [body(): totals = lax.psum_scatter(partial, 'col', scatter_dimension=0, tiled=True)]
    all_gather x1, waiting for transfers between devices: 44 us -> 13.7 us  [body(): piece = lax.all_gather(packed, 'col', axis=0, tiled=True)]
    ppermute x0 -> x22, starting transfers between devices: none -> 26.5 us  [the longest x9 18.5 us: ring_sum(): down = lax.ppermute(down, axis, shifted(size, -1))]
    all_gather x1 -> x0, blocking collectives: 23.2 us -> none  [body(): factors = lax.all_gather(own_factors, 'row', axis=0, tiled=True)]
    all_to_all x1 -> x3, starting transfers between devices: 10 us -> 25.6 us  [the longest x1 11.1 us: body(): lax.all_to_all(jnp.broadcast_to(own_factors[None], (row_count,) + own_fac...]
    dot_general x7 -> x3, matrix products: 14.9 us -> 0.68 us  [matrix_multiply(): return jnp.dot(left, right, preferred_element_type=jnp.float32)]
    ppermute x0 -> x22, waiting for transfers between devices: none -> 9.31 us  [the longest x12 9.28 us: ring_sum(): up = lax.ppermute(up, axis, shifted(size, 1))]
    dot_general x9 -> x10, matrix products: 20.2 us -> 24.3 us  [multiply_right_transposed(): lax.dot_general(left, right, (((1,), (1,)), ((), ())), preferred_element_...]
  transfers between devices with their start and end apart: 4 -> 27, of which waited for: 4 -> 11; matrix products, arithmetic and copies ran while one was open for 3% -> 14% of each run, Pallas kernels for 0% -> 0%
where the time goes in v2:
time: 220 us; the launch traced here: 219 us
  waiting for transfers between devices  103 us (47%)
  starting transfers between devices  52.2 us (24%)
  matrix products  31.9 us (14%)
  between operations  14.5 us (7%)
  local copies, waits for them, and re-layouts  13.8 us (6%)
  other arithmetic  3.68 us (2%)
    all_gather x1, waiting for transfers between devices, body(): lax.all_gather(jnp.concatenate([activations, output_gradient], axis=1), '...  57.6 us
    dot_general x10, matrix products, multiply_right_transposed(): lax.dot_general(left, right, (((1,), (1,)), ((), ())), preferred_element_...  24.3 us
    ppermute x9, starting transfers between devices, ring_sum(): down = lax.ppermute(down, axis, shifted(size, -1))  18.5 us
    all_gather x1, waiting for transfers between devices, body(): piece = lax.all_gather(packed, 'col', axis=0, tiled=True)  13.7 us
    all_to_all x1, waiting for transfers between devices, body(): lax.all_to_all(share, 'row', 0, 0, axis_index_groups=[[2 * chip + c for c...  11.9 us
    all_to_all x1, starting transfers between devices, body(): lax.all_to_all(jnp.broadcast_to(own_factors[None], (row_count,) + own_fac...  11.1 us
    all_to_all x1, waiting for transfers between devices, body(): lax.all_to_all(jnp.broadcast_to(own_factors[None], (row_count,) + own_fac...  10.6 us
    ppermute x12, waiting for transfers between devices, ring_sum(): up = lax.ppermute(up, axis, shifted(size, 1))  9.28 us
  transfers between devices with their start and end apart: 27, of which 11 were waited for; matrix products, arithmetic and copies ran while one was open for 14% of the time, Pallas kernels for 0%

profile of v2, /device:TPU:1, one launch (start us, length us, event | category | flops | bytes accessed | tf_op | source)
XLA Modules:
  0.0 219.2 jit_solution(13402801281925980640)
XLA Ops:
  8.9 57.6 %all-gather.3.cloned.1.call-done = bf16[512,4096]{1,0:T(8,128)(2,1)} async-done(((bf16[16,4096]{1,0:T(8,128)(2,1)}), bf16[512,4096]{1,0:T(8,128)(2,1)}) %all-gather.3.cloned.1.call-update) | async-done | bytes 4194320 | tf_op jit(solution)/shard_map/all_gather | solution.py:88
  66.5 5.2 %fusion.8 = f32[512,896]{1,0:T(8,128)S(1)} fusion(bf16[2048,64]{0,1:T(8,128)(2,1)} %param.16, bf16[2048,832]{0,1:T(8,128)(2,1)} %param.13, bf16[512,4096]{1,0:T(8,128)(2,1)} %all-gather.3.cloned.1.call-done), kind=kOutput, calls=%fused_computation.8 | convolution fusion | flops 1886388224 | bytes 7602176 | tf_op jit(solution)/shard_map/dot_general | solution.py:14
  73.1 1.9 collective-permute-start.18
  74.9 2.4 %fusion = f32[512,896]{1,0:T(8,128)S(1)} fusion(bf16[64,2048]{1,0:T(8,128)(2,1)S(1)} %copy-done.11, bf16[832,2048]{1,0:T(8,128)(2,1)S(1)} %copy-done.10, bf16[512,4096]{1,0:T(8,128)(2,1)S(1)} %copy-done.2), kind=kOutput, calls=%fused_computation | convolution fusion | flops 1886388224 | bytes 7602176 | tf_op jit(solution)/shard_map/dot_general | solution.py:14
  77.5 2.7 %collective-permute-start.4 = (bf16[64,896]{1,0:T(8,128)(2,1)S(1)}, bf16[64,896]{1,0:T(8,128)(2,1)S(1)}, u32[]{:S(2)}, u32[]{:S(2)}) collective-permute-start(bf16[64,896]{1,0:T(8,128)(2,1)S(1)} %get-tuple-element.20), channel_id=1, source_target_pairs={{0,7},{1,0},{2,1},{3,2},{4,3},{5,4},{6,5},{7,6},{8,15},{9,8},{10,9... | collective-permute-start | bytes 344072 | tf_op jit(solution)/shard_map/ppermute | solution.py:58
  80.1 2.4 %fusion.4 = f32[512,896]{1,0:T(8,128)S(1)} fusion(bf16[2048,64]{0,1:T(8,128)(2,1)S(1)} %copy-done.8, bf16[2048,832]{0,1:T(8,128)(2,1)S(1)} %copy-done.4, bf16[512,4096]{1,0:T(8,128)(2,1)S(1)} %copy-done.2), kind=kOutput, calls=%fused_computation.4 | convolution fusion | flops 1886388224 | bytes 7602176 | tf_op jit(solution)/shard_map/dot_general | solution.py:14
  82.6 2.7 %collective-permute-start.11 = (bf16[64,896]{1,0:T(8,128)(2,1)S(1)}, bf16[64,896]{1,0:T(8,128)(2,1)S(1)}, u32[]{:S(2)}, u32[]{:S(2)}) collective-permute-start(bf16[64,896]{1,0:T(8,128)(2,1)S(1)} %get-tuple-element.14), channel_id=1, source_target_pairs={{0,7},{1,0},{2,1},{3,2},{4,3},{5,4},{6,5},{7,6},{8,15},{9,8},{10,9... | collective-permute-start | bytes 344072 | tf_op jit(solution)/shard_map/ppermute | solution.py:58
  85.5 2.0 collective-permute-done.7
  94.0 2.7 %collective-permute-start.5 = (bf16[64,896]{1,0:T(8,128)(2,1)S(1)}, bf16[64,896]{1,0:T(8,128)(2,1)S(1)}, u32[]{:S(2)}, u32[]{:S(2)}) collective-permute-start(bf16[64,896]{1,0:T(8,128)(2,1)S(1)} %get-tuple-element.18), channel_id=1, source_target_pairs={{0,7},{1,0},{2,1},{3,2},{4,3},{5,4},{6,5},{7,6},{8,15},{9,8},{10,9... | collective-permute-start | bytes 344072 | tf_op jit(solution)/shard_map/ppermute | solution.py:58
  102.6 2.4 %collective-permute-start.6 = (bf16[64,896]{1,0:T(8,128)(2,1)S(1)}, bf16[64,896]{1,0:T(8,128)(2,1)S(1)}, u32[]{:S(2)}, u32[]{:S(2)}) collective-permute-start(bf16[64,896]{1,0:T(8,128)(2,1)S(1)} %get-tuple-element.16), channel_id=1, source_target_pairs={{0,7},{1,0},{2,1},{3,2},{4,3},{5,4},{6,5},{7,6},{8,15},{9,8},{10,9... | collective-permute-start | bytes 344072 | tf_op jit(solution)/shard_map/ppermute | solution.py:58
  105.2 2.7 %collective-permute-start.13 = (bf16[64,896]{1,0:T(8,128)(2,1)S(1)}, bf16[64,896]{1,0:T(8,128)(2,1)S(1)}, u32[]{:S(2)}, u32[]{:S(2)}) collective-permute-start(bf16[64,896]{1,0:T(8,128)(2,1)S(1)} %get-tuple-element.10), channel_id=1, source_target_pairs={{0,7},{1,0},{2,1},{3,2},{4,3},{5,4},{6,5},{7,6},{8,15},{9,8},{10,9... | collective-permute-start | bytes 344072 | tf_op jit(solution)/shard_map/ppermute | solution.py:58
  108.6 2.6 %collective-permute-done.10 = bf16[64,896]{1,0:T(8,128)(2,1)S(1)} collective-permute-done((bf16[64,896]{1,0:T(8,128)(2,1)S(1)}, bf16[64,896]{1,0:T(8,128)(2,1)S(1)}, u32[]{:S(2)}, u32[]{:S(2)}) %collective-permute-start.10) | collective-permute-done | bytes 114720 | tf_op jit(solution)/shard_map/ppermute | solution.py:56
  114.3 11.1 %all-to-all-start.1 = ((bf16[32,64,192]{2,1,0:T(8,128)(2,1)}), bf16[32,64,192]{2,1,0:T(8,128)(2,1)S(1)}, u32[]{:S(2)}, u32[]{:S(2)}) async-start(bf16[32,64,192]{2,1,0:T(8,128)(2,1)} %broadcast_in_dim.4), calls=%async_computation.1 | async-start | bytes 2097152 | tf_op jit(solution)/shard_map/all_to_all | solution.py:125
  125.4 4.3 %constant_dynamic-update-slice_fusion.1 = bf16[2048,1664]{0,1:T(8,128)(2,1)} fusion(bf16[2048,832]{0,1:T(8,128)(2,1)} %param.13), kind=kLoop, calls=%fused_computation.86 | loop fusion | bytes 6815744
  129.7 2.0 constant_dynamic-update-slice_fusion
  131.7 10.6 %all-to-all-done.1 = bf16[32,64,192]{2,1,0:T(8,128)(2,1)S(1)} async-done(((bf16[32,64,192]{2,1,0:T(8,128)(2,1)}), bf16[32,64,192]{2,1,0:T(8,128)(2,1)S(1)}, u32[]{:S(2)}, u32[]{:S(2)}) %all-to-all-start.1) | async-done | bytes 786464 | tf_op jit(solution)/shard_map/all_to_all | solution.py:125
  143.2 7.1 %all-to-all-start.2 = ((bf16[8,64,192]{2,1,0:T(8,128)(2,1)}), bf16[8,64,192]{2,1,0:T(8,128)(2,1)S(1)}, u32[]{:S(2)}, u32[]{:S(2)}) async-start(bf16[8,64,192]{2,1,0:T(8,128)(2,1)} %broadcast_in_dim.5), calls=%async_computation.2 | async-start | bytes 524288 | tf_op jit(solution)/shard_map/all_to_all | solution.py:133
  150.3 13.7 %all-gather.5.cloned.1.call-done = bf16[512,2688]{1,0:T(8,128)(2,1)} async-done(((bf16[64,2688]{1,0:T(8,128)(2,1)}), bf16[512,2688]{1,0:T(8,128)(2,1)}) %all-gather.5.cloned.1.call-update) | async-done | bytes 2752528 | tf_op jit(solution)/shard_map/all_gather | solution.py:115
  166.6 6.1 %convolution_convert_fusion = bf16[256,2048]{1,0:T(8,128)(2,1)} fusion(bf16[256,1664]{1,0:T(8,128)(2,1)S(1)} %bitcast.28, bf16[2048,1664]{0,1:T(8,128)(2,1)} %constant_dynamic-update-slice_fusion), kind=kOutput, calls=%fused_computation.12 | convolution fusion | flops 1745354752 | bytes 8716288 | tf_op jit(solution)/shard_map/dot_general | solution.py:14
  172.7 2.4 %collective-permute-start.21 = (bf16[256,2048]{1,0:T(8,128)(2,1)}, bf16[256,2048]{1,0:T(8,128)(2,1)}, u32[]{:S(2)}, u32[]{:S(2)}) collective-permute-start(bf16[256,2048]{1,0:T(8,128)(2,1)} %convolution_convert_fusion), channel_id=1, source_target_pairs={{0,8},{8,0},{16,24},{24,16},{32,40},{40,32},{48,56},{56,48},{64,72... | collective-permute-start | bytes 3145736 | tf_op jit(solution)/shard_map/ppermute | solution.py:149
  175.1 1.9 fusion.40
  179.1 6.6 %add_convert_fusion = bf16[256,2048]{1,0:T(8,128)(2,1)} fusion(bf16[256,2048]{1,0:T(8,128)(2,1)} %collective-permute-done.21, bf16[256,1664]{1,0:T(8,128)(2,1)} %bitcast.27, bf16[2048,1664]{0,1:T(8,128)(2,1)} %constant_dynamic-update-slice_fusion), kind=kOutput, calls=%fused_computation.18 | convolution fusion | flops 1746403328 | bytes 9764864 | tf_op jit(solution)/shard_map/dot_general | solution.py:14
  185.7 7.4 %all-to-all-start = ((bf16[16,16,2048]{2,1,0:T(8,128)(2,1)}), bf16[16,16,2048]{2,1,0:T(8,128)(2,1)}, u32[]{:S(2)}, u32[]{:S(2)}) async-start(bf16[16,16,2048]{2,1,0:T(8,128)(2,1)} %bitcast.26), calls=%async_computation | async-start | bytes 2097152 | tf_op jit(solution)/shard_map/all_to_all | solution.py:152
  198.3 11.9 %all-to-all-done = bf16[16,16,2048]{2,1,0:T(8,128)(2,1)} async-done(((bf16[16,16,2048]{2,1,0:T(8,128)(2,1)}), bf16[16,16,2048]{2,1,0:T(8,128)(2,1)}, u32[]{:S(2)}, u32[]{:S(2)}) %all-to-all-start) | async-done | bytes 1048608 | tf_op jit(solution)/shard_map/all_to_all | solution.py:152
  (106 shorter events, 32.5 us)
Async XLA Ops:
  7.2 59.3 %all-gather.3.cloned.1.call-start = ((), (), s32[]{:S(2)}) async-start(), calls=%async_computation.3 | async-start | bytes 4325376 | tf_op jit(solution)/shard_map/all_gather | solution.py:88
  8.8 155.3 %all-gather.5.cloned.1.call-start = ((), (), s32[]{:S(2)}) async-start(), calls=%async_computation.4 | async-start | bytes 3096576 | tf_op jit(solution)/shard_map/all_gather | solution.py:115
  71.7 10.9 %collective-permute-start.14 = (bf16[64,896]{1,0:T(8,128)(2,1)S(1)}, bf16[64,896]{1,0:T(8,128)(2,1)S(1)}, u32[]{:S(2)}, u32[]{:S(2)}) collective-permute-start(bf16[64,896]{1,0:T(8,128)(2,1)S(1)} %get-tuple-element.25), channel_id=1, source_target_pairs={{0,1},{1,2},{2,3},{3,4},{4,5},{5,6},{6,7},{7,0},{8,9},{9,10},{10,1... | collective-permute-start | bytes 344072 | tf_op jit(solution)/shard_map/ppermute | solution.py:56
  73.1 14.4 %collective-permute-start.18 = (bf16[64,896]{1,0:T(8,128)(2,1)S(1)}, bf16[64,896]{1,0:T(8,128)(2,1)S(1)}, u32[]{:S(2)}, u32[]{:S(2)}) collective-permute-start(bf16[64,896]{1,0:T(8,128)(2,1)S(1)} %get-tuple-element.26), channel_id=1, source_target_pairs={{0,7},{1,0},{2,1},{3,2},{4,3},{5,4},{6,5},{7,6},{8,15},{9,8},{10,9... | collective-permute-start | bytes 344072 | tf_op jit(solution)/shard_map/ppermute | solution.py:58
  77.4 8.0 %collective-permute-start = (bf16[64,896]{1,0:T(8,128)(2,1)S(1)}, bf16[64,896]{1,0:T(8,128)(2,1)S(1)}, u32[]{:S(2)}, u32[]{:S(2)}) collective-permute-start(bf16[64,896]{1,0:T(8,128)(2,1)S(1)} %get-tuple-element.19), channel_id=1, source_target_pairs={{0,1},{1,2},{2,3},{3,4},{4,5},{5,6},{6,7},{7,0},{8,9},{9,10},{10,1... | collective-permute-start | bytes 344072 | tf_op jit(solution)/shard_map/ppermute | solution.py:56
  77.5 14.4 %collective-permute-start.4 = (bf16[64,896]{1,0:T(8,128)(2,1)S(1)}, bf16[64,896]{1,0:T(8,128)(2,1)S(1)}, u32[]{:S(2)}, u32[]{:S(2)}) collective-permute-start(bf16[64,896]{1,0:T(8,128)(2,1)S(1)} %get-tuple-element.20), channel_id=1, source_target_pairs={{0,7},{1,0},{2,1},{3,2},{4,3},{5,4},{6,5},{7,6},{8,15},{9,8},{10,9... | collective-permute-start | bytes 344072 | tf_op jit(solution)/shard_map/ppermute | solution.py:58
  82.6 11.3 %collective-permute-start.11 = (bf16[64,896]{1,0:T(8,128)(2,1)S(1)}, bf16[64,896]{1,0:T(8,128)(2,1)S(1)}, u32[]{:S(2)}, u32[]{:S(2)}) collective-permute-start(bf16[64,896]{1,0:T(8,128)(2,1)S(1)} %get-tuple-element.14), channel_id=1, source_target_pairs={{0,7},{1,0},{2,1},{3,2},{4,3},{5,4},{6,5},{7,6},{8,15},{9,8},{10,9... | collective-permute-start | bytes 344072 | tf_op jit(solution)/shard_map/ppermute | solution.py:58
  87.5 6.3 %collective-permute-start.1 = (bf16[64,896]{1,0:T(8,128)(2,1)S(1)}, bf16[64,896]{1,0:T(8,128)(2,1)S(1)}, u32[]{:S(2)}, u32[]{:S(2)}) collective-permute-start(bf16[64,896]{1,0:T(8,128)(2,1)S(1)} %add_convert_fusion.15), channel_id=1, source_target_pairs={{0,1},{1,2},{2,3},{3,4},{4,5},{5,6},{6,7},{7,0},{8,9},{9,10},{10,1... | collective-permute-start | bytes 344072 | tf_op jit(solution)/shard_map/ppermute | solution.py:56
  87.5 9.1 %collective-permute-start.8 = (bf16[64,896]{1,0:T(8,128)(2,1)S(1)}, bf16[64,896]{1,0:T(8,128)(2,1)S(1)}, u32[]{:S(2)}, u32[]{:S(2)}) collective-permute-start(bf16[64,896]{1,0:T(8,128)(2,1)S(1)} %add_convert_fusion.10), channel_id=1, source_target_pairs={{0,1},{1,2},{2,3},{3,4},{4,5},{5,6},{6,7},{7,0},{8,9},{9,10},{10,1... | collective-permute-start | bytes 344072 | tf_op jit(solution)/shard_map/ppermute | solution.py:56
  90.3 8.1 %collective-permute-start.16 = (bf16[64,896]{1,0:T(8,128)(2,1)S(1)}, bf16[64,896]{1,0:T(8,128)(2,1)S(1)}, u32[]{:S(2)}, u32[]{:S(2)}) collective-permute-start(bf16[64,896]{1,0:T(8,128)(2,1)S(1)} %get-tuple-element.23), channel_id=1, source_target_pairs={{0,1},{1,2},{2,3},{3,4},{4,5},{5,6},{6,7},{7,0},{8,9},{9,10},{10,1... | collective-permute-start | bytes 344072 | tf_op jit(solution)/shard_map/ppermute | solution.py:56
  91.8 7.6 %collective-permute-start.19 = (bf16[64,896]{1,0:T(8,128)(2,1)S(1)}, bf16[64,896]{1,0:T(8,128)(2,1)S(1)}, u32[]{:S(2)}, u32[]{:S(2)}) collective-permute-start(bf16[64,896]{1,0:T(8,128)(2,1)S(1)} %get-tuple-element.24), channel_id=1, source_target_pairs={{0,7},{1,0},{2,1},{3,2},{4,3},{5,4},{6,5},{7,6},{8,15},{9,8},{10,9... | collective-permute-start | bytes 344072 | tf_op jit(solution)/shard_map/ppermute | solution.py:58
  93.9 7.0 %collective-permute-start.2 = (bf16[64,896]{1,0:T(8,128)(2,1)S(1)}, bf16[64,896]{1,0:T(8,128)(2,1)S(1)}, u32[]{:S(2)}, u32[]{:S(2)}) collective-permute-start(bf16[64,896]{1,0:T(8,128)(2,1)S(1)} %get-tuple-element.17), channel_id=1, source_target_pairs={{0,1},{1,2},{2,3},{3,4},{4,5},{5,6},{6,7},{7,0},{8,9},{9,10},{10,1... | collective-permute-start | bytes 344072 | tf_op jit(solution)/shard_map/ppermute | solution.py:56
  94.0 8.3 %collective-permute-start.5 = (bf16[64,896]{1,0:T(8,128)(2,1)S(1)}, bf16[64,896]{1,0:T(8,128)(2,1)S(1)}, u32[]{:S(2)}, u32[]{:S(2)}) collective-permute-start(bf16[64,896]{1,0:T(8,128)(2,1)S(1)} %get-tuple-element.18), channel_id=1, source_target_pairs={{0,7},{1,0},{2,1},{3,2},{4,3},{5,4},{6,5},{7,6},{8,15},{9,8},{10,9... | collective-permute-start | bytes 344072 | tf_op jit(solution)/shard_map/ppermute | solution.py:58
  96.7 6.0 %collective-permute-start.9 = (bf16[64,896]{1,0:T(8,128)(2,1)S(1)}, bf16[64,896]{1,0:T(8,128)(2,1)S(1)}, u32[]{:S(2)}, u32[]{:S(2)}) collective-permute-start(bf16[64,896]{1,0:T(8,128)(2,1)S(1)} %get-tuple-element.11), channel_id=1, source_target_pairs={{0,1},{1,2},{2,3},{3,4},{4,5},{5,6},{6,7},{7,0},{8,9},{9,10},{10,1... | collective-permute-start | bytes 344072 | tf_op jit(solution)/shard_map/ppermute | solution.py:56
  98.4 6.6 %collective-permute-start.12 = (bf16[64,896]{1,0:T(8,128)(2,1)S(1)}, bf16[64,896]{1,0:T(8,128)(2,1)S(1)}, u32[]{:S(2)}, u32[]{:S(2)}) collective-permute-start(bf16[64,896]{1,0:T(8,128)(2,1)S(1)} %get-tuple-element.12), channel_id=1, source_target_pairs={{0,7},{1,0},{2,1},{3,2},{4,3},{5,4},{6,5},{7,6},{8,15},{9,8},{10,9... | collective-permute-start | bytes 344072 | tf_op jit(solution)/shard_map/ppermute | solution.py:58
  99.5 5.7 %collective-permute-start.17 = (bf16[64,896]{1,0:T(8,128)(2,1)S(1)}, bf16[64,896]{1,0:T(8,128)(2,1)S(1)}, u32[]{:S(2)}, u32[]{:S(2)}) collective-permute-start(bf16[64,896]{1,0:T(8,128)(2,1)S(1)} %get-tuple-element.21), channel_id=1, source_target_pairs={{0,1},{1,2},{2,3},{3,4},{4,5},{5,6},{6,7},{7,0},{8,9},{9,10},{10,1... | collective-permute-start | bytes 344072 | tf_op jit(solution)/shard_map/ppermute | solution.py:56
  100.9 7.0 %collective-permute-start.20 = (bf16[64,896]{1,0:T(8,128)(2,1)S(1)}, bf16[64,896]{1,0:T(8,128)(2,1)S(1)}, u32[]{:S(2)}, u32[]{:S(2)}) collective-permute-start(bf16[64,896]{1,0:T(8,128)(2,1)S(1)} %get-tuple-element.22), channel_id=1, source_target_pairs={{0,7},{1,0},{2,1},{3,2},{4,3},{5,4},{6,5},{7,6},{8,15},{9,8},{10,9... | collective-permute-start | bytes 344072 | tf_op jit(solution)/shard_map/ppermute | solution.py:58
  102.3 5.9 %collective-permute-start.3 = (bf16[64,896]{1,0:T(8,128)(2,1)S(1)}, bf16[64,896]{1,0:T(8,128)(2,1)S(1)}, u32[]{:S(2)}, u32[]{:S(2)}) collective-permute-start(bf16[64,896]{1,0:T(8,128)(2,1)S(1)} %get-tuple-element.15), channel_id=1, source_target_pairs={{0,1},{1,2},{2,3},{3,4},{4,5},{5,6},{6,7},{7,0},{8,9},{9,10},{10,1... | collective-permute-start | bytes 344072 | tf_op jit(solution)/shard_map/ppermute | solution.py:56
  105.1 6.1 %collective-permute-start.10 = (bf16[64,896]{1,0:T(8,128)(2,1)S(1)}, bf16[64,896]{1,0:T(8,128)(2,1)S(1)}, u32[]{:S(2)}, u32[]{:S(2)}) collective-permute-start(bf16[64,896]{1,0:T(8,128)(2,1)S(1)} %get-tuple-element.9), channel_id=1, source_target_pairs={{0,1},{1,2},{2,3},{3,4},{4,5},{5,6},{6,7},{7,0},{8,9},{9,10},{10,1... | collective-permute-start | bytes 344072 | tf_op jit(solution)/shard_map/ppermute | solution.py:56
  105.2 6.0 %collective-permute-start.13 = (bf16[64,896]{1,0:T(8,128)(2,1)S(1)}, bf16[64,896]{1,0:T(8,128)(2,1)S(1)}, u32[]{:S(2)}, u32[]{:S(2)}) collective-permute-start(bf16[64,896]{1,0:T(8,128)(2,1)S(1)} %get-tuple-element.10), channel_id=1, source_target_pairs={{0,7},{1,0},{2,1},{3,2},{4,3},{5,4},{6,5},{7,6},{8,15},{9,8},{10,9... | collective-permute-start | bytes 344072 | tf_op jit(solution)/shard_map/ppermute | solution.py:58
  114.3 28.0 %all-to-all-start.1 = ((bf16[32,64,192]{2,1,0:T(8,128)(2,1)}), bf16[32,64,192]{2,1,0:T(8,128)(2,1)S(1)}, u32[]{:S(2)}, u32[]{:S(2)}) async-start(bf16[32,64,192]{2,1,0:T(8,128)(2,1)} %broadcast_in_dim.4), calls=%async_computation.1 | async-start | bytes 2097152 | tf_op jit(solution)/shard_map/all_to_all | solution.py:125
  143.2 33.9 %all-to-all-start.2 = ((bf16[8,64,192]{2,1,0:T(8,128)(2,1)}), bf16[8,64,192]{2,1,0:T(8,128)(2,1)S(1)}, u32[]{:S(2)}, u32[]{:S(2)}) async-start(bf16[8,64,192]{2,1,0:T(8,128)(2,1)} %broadcast_in_dim.5), calls=%async_computation.2 | async-start | bytes 524288 | tf_op jit(solution)/shard_map/all_to_all | solution.py:133
  172.7 6.4 %collective-permute-start.21 = (bf16[256,2048]{1,0:T(8,128)(2,1)}, bf16[256,2048]{1,0:T(8,128)(2,1)}, u32[]{:S(2)}, u32[]{:S(2)}) collective-permute-start(bf16[256,2048]{1,0:T(8,128)(2,1)} %convolution_convert_fusion), channel_id=1, source_target_pairs={{0,8},{8,0},{16,24},{24,16},{32,40},{40,32},{48,56},{56,48},{64,72... | collective-permute-start | bytes 3145736 | tf_op jit(solution)/shard_map/ppermute | solution.py:149
  185.7 24.5 %all-to-all-start = ((bf16[16,16,2048]{2,1,0:T(8,128)(2,1)}), bf16[16,16,2048]{2,1,0:T(8,128)(2,1)}, u32[]{:S(2)}, u32[]{:S(2)}) async-start(bf16[16,16,2048]{2,1,0:T(8,128)(2,1)} %bitcast.26), calls=%async_computation | async-start | bytes 2097152 | tf_op jit(solution)/shard_map/all_to_all | solution.py:152
  (16 other events, 285.0 us)
Sparse Core Ops, SparseCore 0:
  11.1 55.2 all-gather.2
  112.7 51.3 all-gather.4
